TPU v7x, 512 devices: a whole 4x8x8 slice. The times are simulated.
512 devices in a mesh: dp: 16 (over y, x_lo), comp: 32 (over z, x_hi, core).
Axes of the slice: x: 4 (x_hi: 2, x_lo: 2; x = x_hi * 2 + x_lo), y: 8, z: 8, core: 2. Of those that a mesh axis runs over, the one named last changes fastest.
Arguments:
- descriptors: float32 [32768, 128], P(('dp', 'comp')), may hold values from -10 to 10
- means: float32 [128, 16384], P(None, 'comp'), may hold values from -0.8 to 0.8
- variances: float32 [128, 16384], P(None, 'comp'), may hold values from 0.25 to 2
- log_weights: float32 [16384], P('comp'), may hold values from -3 to 0
Outputs:
- new_means: float32 [128, 16384], P('dp', 'comp')
- new_variances: float32 [128, 16384], P('dp', 'comp')
- new_log_weights: float32 [16384], P('comp')
- mean_loglik: float32 [], replicated
All inputs are finite; a program needn't handle non-finite values.
Results may differ from a plain program's by a relative error of at most 0.0003.
Values sent between devices are 32-bit elements; how exact they have to be, the bound alone decides.
A program may use at most 64 MiB of HBM per device.

v0:
```python
import math
import jax
import jax.numpy as jnp
from jax import lax
from jax.sharding import PartitionSpec as P

LOG_TWO_PI = math.log(2.0 * math.pi)
PRIOR = 1.0


def matmul(left, right):
    return jnp.dot(left, right, precision=lax.Precision.HIGHEST, preferred_element_type=jnp.float32)


def local(descriptors, means, variances, log_weights):
    dims = means.shape[0]
    precision_mat = 1.0 / variances
    linear = means * precision_mat
    offset = (
        log_weights
        - 0.5 * jnp.sum(means * linear, 0)
        - 0.5 * jnp.sum(jnp.log(variances), 0)
        - 0.5 * dims * LOG_TWO_PI
    )
    local_rows = descriptors.shape[0]
    groups = lax.axis_size("comp")
    gathered_rows = local_rows * groups
    blocks = max(1, gathered_rows // 1024)
    block_size = gathered_rows // blocks
    comp_local = means.shape[1]
    gathered = lax.all_gather(descriptors, "comp", axis=0, tiled=True)
    counts = jnp.zeros((comp_local,), jnp.float32)
    first = jnp.zeros((dims, comp_local), jnp.float32)
    second = jnp.zeros((dims, comp_local), jnp.float32)
    loglik = jnp.zeros((), jnp.float32)
    for number in range(blocks):
        rows = gathered[number * block_size : (number + 1) * block_size]
        squares = rows * rows
        scores = -0.5 * matmul(squares, precision_mat) + matmul(rows, linear) + offset
        top = lax.pmax(jnp.max(scores, 1), "comp")
        total = lax.psum(jnp.sum(jnp.exp(scores - top[:, None]), 1), "comp")
        norm = top + jnp.log(total)
        resp = jnp.exp(scores - norm[:, None])
        counts = counts + jnp.sum(resp, 0)
        first = first + matmul(rows.T, resp)
        second = second + matmul(squares.T, resp)
        loglik = loglik + jnp.sum(norm)
    first_part, second_part = (
        lax.psum_scatter(first, "dp", scatter_dimension=0, tiled=True),
        lax.psum_scatter(second, "dp", scatter_dimension=0, tiled=True),
    )
    counts, loglik = lax.psum((counts, loglik), "dp")
    owned = first_part.shape[0]
    start = lax.axis_index("dp") * owned
    means_part = lax.dynamic_slice_in_dim(means, start, owned, 0)
    variances_part = lax.dynamic_slice_in_dim(variances, start, owned, 0)
    denom = counts + PRIOR
    new_means = (first_part + PRIOR * means_part) / denom
    scatter = second_part - 2.0 * means_part * first_part + means_part * means_part * counts
    new_variances = (scatter + PRIOR * variances_part) / denom
    total_rows = gathered_rows * lax.axis_size("dp")
    all_comps = comp_local * groups
    new_log_weights = jnp.log((counts + PRIOR) / (total_rows + all_comps * PRIOR))
    mean_loglik = loglik / (total_rows * dims)
    return (new_means, new_variances, new_log_weights, mean_loglik)


def solution(mesh):
    placed = (P(("dp", "comp"), None), P(None, "comp"), P(None, "comp"), P("comp"))
    return jax.shard_map(
        local,
        mesh=mesh,
        in_specs=placed,
        out_specs=(P("dp", "comp"), P("dp", "comp"), P("comp"), P()),
        check_vma=False,
    )
```

profile of v0, /device:TPU:4, one launch (start us, length us, event | category | flops | bytes accessed | tf_op | source)
XLA Modules:
  0.0 405.1 jit_solution(15663945424928719993)
XLA Ops:
  8.0 0.7 constant_dynamic-slice_fusion
  8.7 0.8 copy.23
  9.5 0.9 copy.24
  10.4 1.1 multiply_reduce_fusion
  12.2 85.8 %all-gather.2.cloned.1.call-done = f32[2048,128]{1,0:T(8,128)} async-done(((f32[64,128]{1,0:T(8,128)}), f32[2048,128]{1,0:T(8,128)}) %all-gather.2.cloned.1.call-update) | async-done | bytes 1048592 | tf_op jit(solution)/shard_map/all_gather | solution.py:31
  98.0 3.0 fusion.19
  101.1 1.8 fusion.16
  103.0 2.2 fusion.33
  105.1 3.5 fusion.34
  108.6 64.2 %all-reduce.1 = (f32[1024]{0:T(1024)S(1)}, f32[1024]{0:T(1024)S(1)}) all-reduce(f32[1024]{0:T(1024)S(1)} %get-tuple-element.28, f32[1024]{0:T(1024)S(1)} %get-tuple-element.30), channel_id=1, replica_groups=mesh['dp'=16,'comp'=32] {'comp'}, use_global_device_ids=true, to_apply=%region_3.0 | all-reduce | flops 2048 | bytes 16384 | tf_op jit(solution)/shard_map/pmax | solution.py:40
  172.9 1.9 exponential_reduce_fusion
  175.1 66.2 %all-reduce = (f32[1024]{0:T(1024)S(1)}, f32[1024]{0:T(1024)S(1)}) all-reduce(f32[1024]{0:T(1024)S(1)} %exponential_reduce_fusion.1, f32[1024]{0:T(1024)S(1)} %exponential_reduce_fusion), channel_id=1, replica_groups=mesh['dp'=16,'comp'=32] {'comp'}, use_global_device_ids=true, to_apply=%region_5.0 | all-reduce | flops 2048 | bytes 16384 | tf_op jit(solution)/shard_map/psum | solution.py:41
  241.9 1.9 fusion.4
  243.8 1.9 fusion.9
  245.7 0.9 copy.19
  246.6 2.5 fusion.2
  249.2 3.2 fusion.10
  252.4 2.0 fusion.6
  256.1 35.2 %all-reduce.2 = (f32[512]{0:T(512)S(1)}, f32[]{:T(128)}) all-reduce(f32[512]{0:T(512)S(1)} %add.82, f32[]{:T(128)S(6)} %add.87), channel_id=1, replica_groups=mesh['dp'=16,'comp'=32] {'dp'}, use_global_device_ids=true, to_apply=%region_13.0 | all-reduce | flops 513 | bytes 4104 | tf_op jit(solution)/shard_map/psum | solution.py:52
  292.5 28.4 %reduce-scatter.7.cloned.1.call-done = f32[8,512]{1,0:T(8,128)} async-done(((f32[128,512]{1,0:T(8,128)}), f32[8,512]{1,0:T(8,128)}) %reduce-scatter.7.cloned.1.call-update) | async-done | bytes 16400
  320.9 0.8 copy.20
  321.8 73.2 %reduce-scatter.9.cloned.1.call-done = f32[8,512]{1,0:T(8,128)} async-done(((f32[128,512]{1,0:T(8,128)}), f32[8,512]{1,0:T(8,128)}) %reduce-scatter.9.cloned.1.call-update) | async-done | bytes 16400
  395.0 0.8 copy.22
  396.1 0.7 copy.17
  (28 shorter events, 4.4 us)
Async XLA Ops:
  7.2 93.9 %copy-start.3 = (f32[128,512]{1,0:T(8,128)S(1)}, f32[128,512]{1,0:T(8,128)}, u32[]{:S(2)}) copy-start(f32[128,512]{1,0:T(8,128)} %param.6) | copy-start | bytes 786436
  7.2 90.8 %all-gather.2.cloned.1.call-start = ((), (), s32[]{:S(2)}) async-start(), calls=%async_computation.2 | async-start | bytes 1081344 | tf_op jit(solution)/shard_map/all_gather | solution.py:31
  7.9 313.0 %reduce-scatter.7.cloned.1.call-start = ((), (), s32[]{:S(2)}) async-start(), calls=%async_computation.3 | async-start | bytes 278528
  98.0 3.0 copy-start.2
  101.1 1.9 copy-start.4
  241.3 2.5 copy-start
  246.6 148.4 %reduce-scatter.9.cloned.1.call-start = ((), (), s32[]{:S(2)}) async-start(), calls=%async_computation.4 | async-start | bytes 278528
  246.6 2.5 copy-start.1
  252.4 143.4 %copy-start.5 = (f32[8,512]{0,1:T(8,128)S(1)}, f32[8,512]{0,1:T(8,128)}, u32[]{:S(2)}) copy-start(f32[8,512]{0,1:T(8,128)} %copy.23) | copy-start | bytes 49156
  252.4 143.4 %copy-start.6 = (f32[8,512]{0,1:T(8,128)S(1)}, f32[8,512]{0,1:T(8,128)}, u32[]{:S(2)}) copy-start(f32[8,512]{0,1:T(8,128)} %copy.24) | copy-start | bytes 49156
Sparse Core Ops, SparseCore 0:
  11.4 86.5 all-gather.1
  246.7 74.1 reduce-scatter.6
  324.0 70.9 reduce-scatter.8
where the time goes:
time: 406 us; the launch traced here: 405 us
  waiting for transfers between devices  188 us (46%)
  blocking collectives  166 us (41%)
  matrix products  20 us (5%)
  between operations  17 us (4%)
  other arithmetic  7.85 us (2%)
  local copies, waits for them, and re-layouts  6.41 us (2%)
    unnamed x5, waiting for transfers between devices  102 us
    all_gather x1, waiting for transfers between devices, local(): gathered = lax.all_gather(descriptors, 'comp', axis=0, tiled=True)  85.8 us
    psum x1, blocking collectives, local(): total = lax.psum(jnp.sum(jnp.exp(scores - top[:, None]), 1), 'comp')  66.2 us
    pmax x1, blocking collectives, local(): top = lax.pmax(jnp.max(scores, 1), 'comp')  64.2 us
    psum x1, blocking collectives, local(): counts, loglik = lax.psum((counts, loglik), 'dp')  35.2 us
    dot_general x8, matrix products, matmul(): jnp.dot(left, right, precision=lax.Precision.HIGHEST, preferred_element_t...  20 us
  transfers between devices with their start and end apart: 3, of which 3 were waited for; matrix products, arithmetic and copies ran while one was open for 3% of the time, Pallas kernels for 0%

commit v1 on v0

--- a/solution.py
+++ b/solution.py
@@ -28,7 +28,10 @@
     blocks = max(1, gathered_rows // 1024)
     block_size = gathered_rows // blocks
     comp_local = means.shape[1]
-    gathered = lax.all_gather(descriptors, "comp", axis=0, tiled=True)
+    size = lax.axis_size("comp")
+    pieces = jnp.stack([descriptors for _ in range(size)])
+    pieces = lax.all_to_all(pieces, "comp", split_axis=0, concat_axis=0)
+    gathered = jnp.concatenate(pieces, axis=0)
     counts = jnp.zeros((comp_local,), jnp.float32)
     first = jnp.zeros((dims, comp_local), jnp.float32)
     second = jnp.zeros((dims, comp_local), jnp.float32)

time: 406 us -> 356 us (0.88)
  waiting for transfers between devices: 188 us -> 130 us
  starting transfers between devices: 0.12 us -> 13.5 us
    all_gather x1 -> x0, waiting for transfers between devices: 85.8 us -> none  [local(): gathered = lax.all_gather(descriptors, 'comp', axis=0, tiled=True)]
    all_to_all x0 -> x1, waiting for transfers between devices: none -> 27 us  [local(): pieces = lax.all_to_all(pieces, 'comp', split_axis=0, concat_axis=0)]
    all_to_all x0 -> x1, starting transfers between devices: none -> 13.4 us  [local(): pieces = lax.all_to_all(pieces, 'comp', split_axis=0, concat_axis=0)]
    unnamed x5 -> x4, waiting for transfers between devices: 102 us -> 103 us
where the time goes in v1:
time: 356 us; the launch traced here: 355 us
  blocking collectives  162 us (46%)
  waiting for transfers between devices  130 us (37%)
  matrix products  18.8 us (5%)
  between operations  17.4 us (5%)
  starting transfers between devices  13.5 us (4%)
  local copies, waits for them, and re-layouts  7.67 us (2%)
  other arithmetic  6.14 us (2%)
    unnamed x4, waiting for transfers between devices  103 us
    psum x1, blocking collectives, local(): total = lax.psum(jnp.sum(jnp.exp(scores - top[:, None]), 1), 'comp')  66.2 us
    pmax x1, blocking collectives, local(): top = lax.pmax(jnp.max(scores, 1), 'comp')  60.5 us
    psum x1, blocking collectives, local(): counts, loglik = lax.psum((counts, loglik), 'dp')  35.3 us
    all_to_all x1, waiting for transfers between devices, local(): pieces = lax.all_to_all(pieces, 'comp', split_axis=0, concat_axis=0)  27 us
    dot_general x8, matrix products, matmul(): jnp.dot(left, right, precision=lax.Precision.HIGHEST, preferred_element_t...  18.8 us
    all_to_all x1, starting transfers between devices, local(): pieces = lax.all_to_all(pieces, 'comp', split_axis=0, concat_axis=0)  13.4 us
  transfers between devices with their start and end apart: 3, of which 3 were waited for; matrix products, arithmetic and copies ran while one was open for 3% of the time, Pallas kernels for 0%

profile of v1, /device:TPU:4, one launch (start us, length us, event | category | flops | bytes accessed | tf_op | source)
XLA Modules:
  0.0 355.3 jit_solution(14690133992147197365)
XLA Ops:
  7.2 1.9 stack.2
  9.1 13.4 %all-to-all-start = ((f32[32,64,128]{2,1,0:T(8,128)}), f32[32,64,128]{2,1,0:T(8,128)S(1)}, u32[]{:S(2)}, u32[]{:S(2)}) async-start(f32[32,64,128]{2,1,0:T(8,128)} %stack.2), calls=%async_computation | async-start | bytes 2097152 | tf_op jit(solution)/shard_map/all_to_all | solution.py:33
  22.7 0.8 copy.23
  23.5 0.9 copy.24
  24.5 27.0 %all-to-all-done = f32[32,64,128]{2,1,0:T(8,128)S(1)} async-done(((f32[32,64,128]{2,1,0:T(8,128)}), f32[32,64,128]{2,1,0:T(8,128)S(1)}, u32[]{:S(2)}, u32[]{:S(2)}) %all-to-all-start) | async-done | bytes 1048608 | tf_op jit(solution)/shard_map/all_to_all | solution.py:33
  51.6 1.8 fusion.16
  53.4 1.8 fusion.19
  55.3 3.5 fusion.27
  58.8 2.2 fusion.26
  61.0 60.5 %all-reduce.1 = (f32[1024]{0:T(1024)S(1)}, f32[1024]{0:T(1024)S(1)}) all-reduce(f32[1024]{0:T(1024)S(1)} %get-tuple-element.30, f32[1024]{0:T(1024)S(1)} %get-tuple-element.32), channel_id=1, replica_groups=mesh['dp'=16,'comp'=32] {'comp'}, use_global_device_ids=true, to_apply=%region_3.0 | all-reduce | flops 2048 | bytes 16384 | tf_op jit(solution)/shard_map/pmax | solution.py:43
  121.5 1.9 exponential_reduce_fusion
  123.8 66.2 %all-reduce = (f32[1024]{0:T(1024)S(1)}, f32[1024]{0:T(1024)S(1)}) all-reduce(f32[1024]{0:T(1024)S(1)} %exponential_reduce_fusion.1, f32[1024]{0:T(1024)S(1)} %exponential_reduce_fusion), channel_id=1, replica_groups=mesh['dp'=16,'comp'=32] {'comp'}, use_global_device_ids=true, to_apply=%region_5.0 | all-reduce | flops 2048 | bytes 16384 | tf_op jit(solution)/shard_map/psum | solution.py:44
  190.6 1.9 fusion.4
  192.5 1.9 fusion.9
  194.3 0.9 copy.19
  195.3 2.5 fusion.2
  197.8 3.2 fusion.10
  201.0 2.0 fusion.6
  204.7 35.3 %all-reduce.2 = (f32[512]{0:T(512)S(1)}, f32[]{:T(128)}) all-reduce(f32[512]{0:T(512)S(1)} %add.82, f32[]{:T(128)S(6)} %add.87), channel_id=1, replica_groups=mesh['dp'=16,'comp'=32] {'dp'}, use_global_device_ids=true, to_apply=%region_13.0 | all-reduce | flops 513 | bytes 4104 | tf_op jit(solution)/shard_map/psum | solution.py:55
  241.3 29.5 %reduce-scatter.7.cloned.1.call-done = f32[8,512]{1,0:T(8,128)} async-done(((f32[128,512]{1,0:T(8,128)}), f32[8,512]{1,0:T(8,128)}) %reduce-scatter.7.cloned.1.call-update) | async-done | bytes 16400
  270.8 0.8 copy.20
  271.6 73.2 %reduce-scatter.9.cloned.1.call-done = f32[8,512]{1,0:T(8,128)} async-done(((f32[128,512]{1,0:T(8,128)}), f32[8,512]{1,0:T(8,128)}) %reduce-scatter.9.cloned.1.call-update) | async-done | bytes 16400
  344.8 0.8 copy.22
  345.9 0.7 copy.17
  (31 shorter events, 3.2 us)
Async XLA Ops:
  7.2 15.5 %copy-start.2 = (f32[128,512]{1,0:T(8,128)S(1)}, f32[128,512]{1,0:T(8,128)}, u32[]{:S(2)}) copy-start(f32[128,512]{1,0:T(8,128)} %param.6) | copy-start | bytes 786436
  7.2 15.5 %copy-start.3 = (f32[128,512]{1,0:T(8,128)S(1)}, f32[128,512]{1,0:T(8,128)}, u32[]{:S(2)}) copy-start(f32[128,512]{1,0:T(8,128)} %param.5) | copy-start | bytes 786436
  7.2 17.3 %copy-start.7 = (f32[512]{0:T(512)S(1)}, f32[512]{0:T(512)}, u32[]{:S(2)}) copy-start(f32[512]{0:T(512)} %param.7) | copy-start | bytes 6148
  9.1 42.4 %all-to-all-start = ((f32[32,64,128]{2,1,0:T(8,128)}), f32[32,64,128]{2,1,0:T(8,128)S(1)}, u32[]{:S(2)}, u32[]{:S(2)}) async-start(f32[32,64,128]{2,1,0:T(8,128)} %stack.2), calls=%async_computation | async-start | bytes 2097152 | tf_op jit(solution)/shard_map/all_to_all | solution.py:33
  22.6 248.2 %reduce-scatter.7.cloned.1.call-start = ((), (), s32[]{:S(2)}) async-start(), calls=%async_computation.3 | async-start | bytes 278528
  53.4 1.9 copy-start.4
  190.0 2.5 copy-start
  195.2 149.6 %reduce-scatter.9.cloned.1.call-start = ((), (), s32[]{:S(2)}) async-start(), calls=%async_computation.4 | async-start | bytes 278528
  195.3 2.5 copy-start.1
  201.0 144.6 %copy-start.5 = (f32[8,512]{0,1:T(8,128)S(1)}, f32[8,512]{0,1:T(8,128)}, u32[]{:S(2)}) copy-start(f32[8,512]{0,1:T(8,128)} %copy.23) | copy-start | bytes 49156
  201.0 144.6 %copy-start.6 = (f32[8,512]{0,1:T(8,128)S(1)}, f32[8,512]{0,1:T(8,128)}, u32[]{:S(2)}) copy-start(f32[8,512]{0,1:T(8,128)} %copy.24) | copy-start | bytes 49156
Sparse Core Ops, SparseCore 0:
  195.3 75.3 reduce-scatter.6
  273.8 71.0 reduce-scatter.8
